TPU v7x, 32 devices: a whole 2x2x4 slice. The times are simulated.
32 devices in a mesh: grid: 8 (over z, x), ch: 4 (over y, core).
Axes of the slice: x: 2, y: 2, z: 4, core: 2. Of those that a mesh axis runs over, the one named last changes fastest.
Arguments:
- inputs: bfloat16 [32, 1024, 512], P('grid', None, 'ch'), may hold values from -6 to 6
- w_gate: bfloat16 [512, 512], P(None, 'ch'), may hold values from -0.25 to 0.25
- w_value: bfloat16 [512, 512], P(None, 'ch'), may hold values from -0.25 to 0.25
- short_filter: bfloat16 [2, 3, 3, 512], P(None, None, None, 'ch'), may hold values from -2 to 2
- row_filter: bfloat16 [1024, 512], P(None, 'ch'), may hold values from -0.1875 to 0.1875
- column_filter: bfloat16 [32, 512], P(None, 'ch'), may hold values from -1 to 1
- cotangent: bfloat16 [32, 1024, 512], P('grid', None, 'ch'), may hold values from -6 to 6
Outputs:
- gated: bfloat16 [32, 1024, 512], P('grid', None, 'ch')
- input_grad: bfloat16 [32, 1024, 512], P('grid', None, 'ch')
- gate_grad: float32 [512, 512], P('grid', 'ch')
- value_grad: float32 [512, 512], P('grid', 'ch')
- short_grad: float32 [2, 3, 3, 512], P(None, None, None, 'ch')
- row_grad: float32 [1024, 512], P('grid', 'ch')
- column_grad: float32 [32, 512], P('grid', 'ch')
All inputs are finite; a program needn't handle non-finite values.
Results may differ from a plain program's by a relative error of at most 0.025.
Values may be sent and summed in bfloat16 or wider, within the bound.
A program may use at most 128 MiB of HBM per device.

v0:
```python
import math

import jax
import jax.numpy as jnp
from jax import lax
from jax.sharding import PartitionSpec as P

highest = lax.Precision.HIGHEST


def extended(value, sides, width):
    for axis, dim in sides:
        size, length = (lax.axis_size(axis), value.shape[dim])
        up = [(i, (i + 1) % size) for i in range(size - 1)]
        down = [(j, i) for i, j in up]
        last = lax.slice_in_dim(value, length - width, length, axis=dim)
        initial = lax.slice_in_dim(value, 0, width, axis=dim)
        before = lax.ppermute(last, axis, up)
        after = lax.ppermute(initial, axis, down)
        value = jnp.concatenate([before, value, after], axis=dim)
    return value


def hartley(length):
    position = jnp.arange(length, dtype=jnp.int32)
    product = position[:, None] * position[None, :] % length
    phases = product.astype(jnp.float32) * (2.0 * math.pi / length)
    return jnp.cos(phases) + jnp.sin(phases)


def mirror(values, along):
    leading = lax.slice_in_dim(values, 0, 1, axis=along)
    remainder = lax.slice_in_dim(values, 1, values.shape[along], axis=along)
    return jnp.concatenate([leading, jnp.flip(remainder, along)], axis=along)


def even_odd(spectrum, along):
    reversed_spec = mirror(spectrum, along)
    return (0.5 * (spectrum + reversed_spec), 0.5 * (spectrum - reversed_spec))


def column_forward(row_cols, cas_height, col_even, col_odd):
    spec_rows = jnp.einsum("hwc,hk->kwc", row_cols, cas_height, precision=highest)
    second = spec_rows * col_even[:, None] + mirror(spec_rows, 0) * col_odd[:, None]
    mixed_cols = (
        jnp.einsum("kwc,kh->hwc", second, cas_height, precision=highest) / cas_height.shape[0]
    )
    return (spec_rows, mixed_cols)


def column_backward(grad_cols, spec_rows, cas_height, col_even, col_odd, scale):
    full_height = cas_height.shape[0]
    spec_grad = jnp.einsum("hwc,hk->kwc", grad_cols, cas_height, precision=highest)
    mirrored_grad = mirror(spec_grad, 0)
    back_cols = spec_grad * col_even[:, None] - mirrored_grad * col_odd[:, None]
    grad_row_cols = (
        jnp.einsum("kwc,kh->hwc", back_cols, cas_height, precision=highest) / full_height
    )
    rows_even, rows_odd = even_odd(spec_rows, 0)
    col_term = jnp.sum(spec_grad * rows_even - mirrored_grad * rows_odd, axis=1)
    col_grad = jnp.einsum("kc,km->mc", col_term, cas_height, precision=highest) * (
        scale / full_height
    )
    return (grad_row_cols, col_grad)


def local(inputs, w_gate, w_value, short_filter, row_filter, column_filter, cotangent):
    tile_rows, full_width, channels = inputs.shape
    gathered = lax.all_gather(inputs, "ch", axis=2, tiled=True)
    w_both = jnp.concatenate([w_gate, w_value], axis=1)
    stacked = jnp.einsum(
        "rwd,dc->rwc", gathered, w_both, preferred_element_type=jnp.float32
    ).astype(jnp.bfloat16)
    kernel = jnp.concatenate([short_filter[0], short_filter[1]], axis=-1).astype(jnp.float32)
    framed = extended(stacked, (("grid", 0),), 1)
    framed = jnp.pad(framed, ((0, 0), (1, 1), (0, 0))).astype(jnp.float32)
    featured = jnp.zeros((tile_rows, full_width, 2 * channels), jnp.float32)
    for row_shift in range(3):
        for col_shift in range(3):
            featured = (
                featured
                + kernel[row_shift, col_shift]
                * framed[row_shift : row_shift + tile_rows, col_shift : col_shift + full_width]
            )
    featured = featured.astype(jnp.bfloat16)
    gate_feat = featured[..., :channels].astype(jnp.float32)
    value_bf = featured[..., channels:]
    cas_width = hartley(full_width)
    width_high = cas_width.astype(jnp.bfloat16)
    width_low = (cas_width - width_high.astype(jnp.float32)).astype(jnp.bfloat16)
    spec_b = jnp.einsum("rwc,wk->rkc", value_bf, width_high, preferred_element_type=jnp.float32)
    spec_b = spec_b + jnp.einsum(
        "rwc,wk->rkc", value_bf, width_low, preferred_element_type=jnp.float32
    )
    row_spec = jnp.einsum("mc,mk->kc", row_filter.astype(jnp.float32), cas_width, precision=highest)
    row_even, row_odd = even_odd(row_spec, 0)
    row_mixed = spec_b * row_even + mirror(spec_b, 1) * row_odd
    mix_row = jnp.einsum("rkc,kw->rwc", row_mixed, cas_width, precision=highest) / full_width
    full_height = column_filter.shape[0]
    cas_height = hartley(full_height)
    col_spec = jnp.einsum(
        "mc,mk->kc", column_filter.astype(jnp.float32), cas_height, precision=highest
    )
    col_even, col_odd = even_odd(col_spec, 0)
    scale = 1.0 / math.sqrt(full_height * full_width)
    grad_out = cotangent.astype(jnp.float32)
    grad_mix = grad_out * gate_feat
    row_cols = lax.all_to_all(mix_row, "grid", split_axis=1, concat_axis=0, tiled=True)
    spec_rows, mixed_cols = column_forward(row_cols, cas_height, col_even, col_odd)
    mix_col = lax.all_to_all(mixed_cols, "grid", split_axis=0, concat_axis=1, tiled=True)
    grad_cols = lax.all_to_all(grad_mix, "grid", split_axis=1, concat_axis=0, tiled=True)
    grad_row_cols, col_grad = column_backward(
        grad_cols, spec_rows, cas_height, col_even, col_odd, scale
    )
    grad_row = lax.all_to_all(grad_row_cols, "grid", split_axis=0, concat_axis=1, tiled=True)
    gated = (gate_feat * mix_col).astype(jnp.bfloat16)
    grad_gate = grad_out * mix_col
    spec_gr = jnp.einsum("rwc,wk->rkc", grad_row, cas_width, precision=highest)
    mirrored_gr = mirror(spec_gr, 1)
    back_rows = spec_gr * row_even - mirrored_gr * row_odd
    grad_value = jnp.einsum("rkc,kw->rwc", back_rows, cas_width, precision=highest) / full_width
    value_even, value_odd = even_odd(spec_b, 1)
    row_term = jnp.sum(spec_gr * value_even - mirrored_gr * value_odd, axis=0)
    row_grad = jnp.einsum("kc,km->mc", row_term, cas_width, precision=highest) * (
        scale / full_width
    )
    grad_feat = jnp.concatenate([grad_gate, grad_value], axis=2)
    grad_framed = extended(grad_feat, (("grid", 0),), 1)
    grad_framed = jnp.pad(grad_framed, ((0, 0), (1, 1), (0, 0)))
    back_sum = jnp.zeros((tile_rows, full_width, 2 * channels), jnp.float32)
    short_rows = []
    for row_shift in range(3):
        short_cols = []
        for col_shift in range(3):
            back_sum = (
                back_sum
                + kernel[row_shift, col_shift]
                * grad_framed[
                    2 - row_shift : 2 - row_shift + tile_rows,
                    2 - col_shift : 2 - col_shift + full_width,
                ]
            )
            short_cols.append(
                jnp.sum(
                    grad_feat
                    * framed[row_shift : row_shift + tile_rows, col_shift : col_shift + full_width],
                    axis=(0, 1),
                )
            )
        short_rows.append(jnp.stack(short_cols))
    back_stack = back_sum.astype(jnp.bfloat16)
    short_term = jnp.stack(short_rows).reshape(3, 3, 2, channels).transpose(2, 0, 1, 3) * scale
    short_grad = lax.psum(short_term, "grid")
    weight_term = (
        jnp.einsum("rwd,rwc->dc", gathered, back_stack, preferred_element_type=jnp.float32) * scale
    )
    gate_grad, value_grad, row_share, col_share = (
        lax.psum_scatter(
            weight_term[:, :channels].astype(jnp.bfloat16), "grid", scatter_dimension=0, tiled=True
        ).astype(jnp.float32),
        lax.psum_scatter(
            weight_term[:, channels:].astype(jnp.bfloat16), "grid", scatter_dimension=0, tiled=True
        ).astype(jnp.float32),
        lax.psum_scatter(
            row_grad.astype(jnp.bfloat16), "grid", scatter_dimension=0, tiled=True
        ).astype(jnp.float32),
        lax.psum_scatter(
            col_grad.astype(jnp.bfloat16), "grid", scatter_dimension=0, tiled=True
        ).astype(jnp.float32),
    )
    partial_term = jnp.einsum("rwc,dc->rwd", back_stack, w_both, preferred_element_type=jnp.float32)
    input_grad = lax.psum_scatter(
        partial_term.astype(jnp.bfloat16), "ch", scatter_dimension=2, tiled=True
    )
    return (gated, input_grad, gate_grad, value_grad, short_grad, row_share, col_share)


def solution(mesh):
    return jax.shard_map(
        local,
        mesh=mesh,
        in_specs=(
            P("grid", None, "ch"),
            P(None, "ch"),
            P(None, "ch"),
            P(None, None, None, "ch"),
            P(None, "ch"),
            P(None, "ch"),
            P("grid", None, "ch"),
        ),
        out_specs=(
            P("grid", None, "ch"),
            P("grid", None, "ch"),
            P("grid", "ch"),
            P("grid", "ch"),
            P(None, None, None, "ch"),
            P("grid", "ch"),
            P("grid", "ch"),
        ),
        check_vma=False,
    )
```

profile of v0, /device:TPU:0, one launch (start us, length us, event | category | flops | bytes accessed | tf_op | source)
XLA Modules:
  0.0 752.9 jit_solution(2997577016465480047)
XLA Ops:
  8.1 20.8 %fusion.43 = f32[1024,128]{1,0:T(8,128)S(1)} fusion(bf16[1024,128]{1,0:T(8,128)(2,1)S(1)} %copy-done), kind=kOutput, calls=%fused_computation.93 | convolution fusion | flops 1626341376 | bytes 786432 | tf_op jit(solution)/shard_map/mc,mk->kc/dot_general | solution.py:95
  29.8 17.5 %all-gather.2.cloned.1.call-done = bf16[4,1024,512]{2,1,0:T(8,128)(2,1)} async-done(((bf16[4,1024,128]{2,1,0:T(8,128)(2,1)}), bf16[4,1024,512]{2,1,0:T(8,128)(2,1)}) %all-gather.2.cloned.1.call-update) | async-done | bytes 4194320 | tf_op jit(solution)/shard_map/all_gather | solution.py:69
  47.4 3.5 convert_bitcast_fusion
  51.9 4.2 collective-permute-start
  57.4 2.7 rev.24
  61.5 16.9 %collective-permute-done = bf16[1,1024,256]{1,2,0:T(8,128)(2,1)} collective-permute-done((bf16[1,1024,256]{1,2,0:T(8,128)(2,1)}, bf16[1,1024,256]{1,2,0:T(8,128)(2,1)}, u32[]{:S(2)}, u32[]{:S(2)}) %collective-permute-start) | collective-permute-done | bytes 524320 | tf_op jit(solution)/shard_map/ppermute | solution.py:18
  78.4 3.2 fusion.22
  81.7 7.7 %add_convert_fusion = bf16[4,1024,256]{1,2,0:T(8,128)(2,1)S(1)} fusion(f32[6,1026,256]{1,2,0:T(8,128)S(1)} %fusion.22, f32[256]{0:T(256)S(1)} %bitcast.164, f32[256]{0:T(256)S(1)} %bitcast.150, f32[256]{0:T(256)S(1)} %bitcast.152, f32[256]{0:T(256)S(1)} %bitcast.154, f32[256]{0:T(256)S(1)} %bitcast.156, f32[256]{0:T(256)S(1)} %bitcast.158, ...), kind=kLoop, calls=%fused_computation.55 | loop fusion | flops 18874368 | bytes 39855104 | tf_op jit(solution)/shard_map/convert_element_type | solution.py:85
  90.7 17.4 %fusion.26 = f32[1024,4,128]{2,0,1:T(8,128)S(1)} fusion(bf16[4,1024,256]{1,2,0:T(8,128)(2,1)S(1)} %add_convert_fusion), kind=kOutput, calls=%fused_computation.67 | convolution fusion | flops 1093664768 | bytes 3145728 | tf_op jit(solution)/shard_map/rwc,wk->rkc/dot_general | solution.py:92
  108.1 18.3 %add_bitcast_fusion = f32[4,1024,128]{2,1,0:T(8,128)S(1)} fusion(f32[1024,4,128]{2,0,1:T(8,128)S(1)} %fusion.26, bf16[4,1024,256]{1,2,0:T(8,128)(2,1)} %copy-done.10), kind=kOutput, calls=%fused_computation.90 | convolution fusion | flops 1091043328 | bytes 5242880 | tf_op jit(solution)/shard_map/rwc,wk->rkc/dot_general | solution.py:91
  128.1 17.3 %rev.25 = f32[4,1023,128]{2,1,0:T(8,128)} reverse(f32[4,1023,128]{2,1,0:T(8,128)} %slice.238), dimensions={1} | reverse | bytes 4190208 | tf_op jit(solution)/shard_map/jit(_flip)/rev | solution.py:34
  147.3 30.1 %multiply_bitcast_fusion.1 = f32[4,1024,128]{1,2,0:T(8,128)S(1)} fusion(f32[4,1024,128]{2,1,0:T(8,128)S(1)} %fusion.175), kind=kOutput, calls=%fused_computation.86 | convolution fusion | flops 6458703872 | bytes 4194304 | tf_op jit(solution)/shard_map/rkc,kw->rwc/dot_general | solution.py:98
  179.3 6.8 all-to-all-start
  186.4 48.1 %all-to-all-done = f32[4,1024,128]{2,0,1:T(4,128)S(1)} async-done(((f32[4,1024,128]{2,0,1:T(4,128)}), f32[4,1024,128]{2,0,1:T(4,128)S(1)}, u32[]{:S(2)}, u32[]{:S(2)}) %all-to-all-start) | async-done | bytes 2097184 | tf_op jit(solution)/shard_map/all_to_all | solution.py:108
  239.0 4.0 rev.27
  243.0 3.7 fusion.47
  246.7 2.5 copy.67
  249.3 3.6 all-to-all-start.1
  252.9 2.3 copy.69
  255.2 46.2 %all-to-all-done.1 = f32[32,128,128]{2,1,0:T(8,128)S(1)} async-done(((f32[32,128,128]{2,1,0:T(8,128)}), f32[32,128,128]{2,1,0:T(8,128)S(1)}, u32[]{:S(2)}, u32[]{:S(2)}) %all-to-all-start.1) | async-done | bytes 2097184 | tf_op jit(solution)/shard_map/all_to_all | solution.py:110
  304.9 4.7 convert_multiply_fusion
  311.6 52.3 %all_to_all.72 = f32[4,1024,128]{2,0,1:T(4,128)S(1)} all-to-all(f32[4,1024,128]{2,0,1:T(4,128)S(1)} %copy.70), channel_id=1, replica_groups=mesh['grid'=8,'ch'=4] {'grid'}, dimensions={1} | all-to-all | bytes 4194304 | tf_op jit(solution)/shard_map/all_to_all | solution.py:111
  368.4 3.9 rev.28
  372.3 3.7 fusion.50
  376.1 2.5 copy.72
  378.6 3.6 all-to-all-start.3
  382.3 17.7 %fusion.178 = f32[1024,1024,1]{1,0,2:T(8,128)} fusion(), kind=kLoop, calls=%fused_computation.39.clone.clone.clone.1 | loop fusion | flops 15728640 | bytes 4194304 | tf_op jit(solution)/shard_map/rwc,wk->rkc/dot_general | solution.py:118
  400.0 17.5 %sine_add_fusion.20 = f32[1024,1024]{1,0:T(8,128)} fusion(), kind=kLoop, calls=%fused_computation.52.clone.1.clone.1 | loop fusion | flops 15728640 | bytes 4194304
  417.5 12.6 %all-to-all-done.3 = f32[32,128,128]{2,1,0:T(8,128)S(1)} async-done(((f32[32,128,128]{2,1,0:T(8,128)}), f32[32,128,128]{2,1,0:T(8,128)S(1)}, u32[]{:S(2)}, u32[]{:S(2)}) %all-to-all-start.3) | async-done | bytes 2097184 | tf_op jit(solution)/shard_map/all_to_all | solution.py:115
  432.3 6.8 fusion.53
  441.2 17.1 %rev.29 = f32[4,1023,128]{2,1,0:T(8,128)} reverse(f32[4,1023,128]{2,1,0:T(8,128)} %slice.246), dimensions={1} | reverse | bytes 4190208 | tf_op jit(solution)/shard_map/jit(_flip)/rev | solution.py:34
  458.3 6.0 subtract_reduce_fusion.1
  466.3 9.1 %fusion.41 = f32[1024,512]{0,1:S(1)} fusion(f32[1024,512]{0,1:T(8,128)S(1)} %bitcast.136, f32[1024,1024]{1,0:T(8,128)} %sine_add_fusion.20), kind=kOutput, calls=%fused_computation.91 | convolution fusion | flops 6442450944 | bytes 8388608
  478.6 3.4 collective-permute-start.2
  483.3 25.0 %fusion.64 = bf16[1024,128]{1,0:T(8,128)(2,1)} fusion(f32[1024,128]{1,0:T(8,128)S(1)} %copy-done.19), kind=kOutput, calls=%fused_computation.102 | convolution fusion | flops 1626603520 | bytes 786432 | tf_op jit(solution)/shard_map/kc,km->mc/dot_general | solution.py:124
  508.4 18.3 %collective-permute-done.2 = f32[1,1024,256]{1,2,0:T(8,128)S(1)} collective-permute-done((f32[1,1024,256]{1,2,0:T(8,128)}, f32[1,1024,256]{1,2,0:T(8,128)S(1)}, u32[]{:S(2)}, u32[]{:S(2)}) %collective-permute-start.2) | collective-permute-done | bytes 1048608 | tf_op jit(solution)/shard_map/ppermute | solution.py:18
  526.8 8.8 %select_maximum_fusion = f32[6,1026,256]{1,2,0:T(8,128)} fusion(f32[1,1024,256]{1,2,0:T(8,128)} %collective-permute-done.3, f32[1,1024,256]{1,2,0:T(8,128)S(1)} %collective-permute-done.2, f32[4,1024,128]{1,2,0:T(8,128)S(1)} %multiply_bitcast_fusion, f32[4,1024,128]{1,2,0:T(8,128)} %get-tuple-element.49), kind=kLoop, calls=%fused_computation.2 | loop fusion | flops 15759360 | bytes 12595200 | tf_op jit(solution)/shard_map/concatenate | solution.py:20
  535.6 15.5 %fusion.5 = bf16[4,1024,256]{1,2,0:T(8,128)(2,1)} fusion(f32[6,1026,256]{1,2,0:T(8,128)} %select_maximum_fusion, f32[1,1024,256]{1,2,0:T(8,128)S(1)} %collective-permute-done.2, f32[4,1024,128]{1,2,0:T(8,128)S(1)} %multiply_bitcast_fusion, f32[4,1024,128]{1,2,0:T(8,128)} %get-tuple-element.49, f32[1,1024,256]{1,2,0:T(8,128)} %collective-permute-done.3, ...), kind=kLoop, calls=%fused_computation.19 | loop fusion | flops 24117248 | bytes 33563648 | tf_op jit(solution)/shard_map/convert_element_type | solution.py:151
  551.1 4.1 fusion.66
  556.9 4.9 convolution_convert_fusion
  561.9 8.1 %copy.95 = bf16[4,1024,512]{1,0,2:T(4,128)(2,1)} copy(bf16[4,1024,512]{2,1,0:T(8,128)(2,1)} %convolution_convert_fusion) | data formatting | bytes 8388608
  569.9 6.5 copy.103
  579.7 4.4 subtract_reduce_fusion
  584.3 21.7 %all-reduce.2 = bf16[32,128]{1,0:T(8,128)(2,1)S(1)} all-reduce(bf16[32,128]{1,0:T(8,128)(2,1)S(1)} %fusion.67), channel_id=6, replica_groups=mesh['grid'=8,'ch'=4] {'grid'}, use_global_device_ids=true, to_apply=%region_16.17.clone | all-reduce | flops 4096 | bytes 16384
  606.6 20.1 %multiply_reduce_fusion.7 = (f32[256]{0:T(256)S(1)}, f32[256]{0:T(256)S(1)}, f32[256]{0:T(256)S(1)}, f32[256]{0:T(256)S(1)}, f32[256]{0:T(256)S(1)}, /*index=5*/...) fusion(f32[6,1026,256]{1,2,0:T(8,128)} %copy-done.2, f32[4,1024,128]{1,2,0:T(8,128)S(1)} %multiply_bitcast_fusion, ...), kind=kLoop, calls=%fused_computation.49 | loop fusion | flops 19920640 | bytes 41952256 | tf_op jit(solution)/shard_map/reduce_sum | solution.py:144
  626.7 18.3 %psum.7 = f32[2,3,3,128]{3,0,2,1:T(2,128)} all-reduce(f32[2,3,3,128]{3,0,2,1:T(2,128)S(1)} %fusion.90), channel_id=1, replica_groups=mesh['grid'=8,'ch'=4] {'grid'}, use_global_device_ids=true, to_apply=%region_12.13 | all-reduce | flops 2304 | bytes 18432 | tf_op jit(solution)/shard_map/psum | solution.py:153
  648.0 48.4 %reduce-scatter.17.cloned.1.call-done = bf16[64,128]{1,0:T(8,128)(2,1)} async-done(((bf16[512,128]{1,0:T(8,128)(2,1)}), bf16[64,128]{1,0:T(8,128)(2,1)}) %reduce-scatter.17.cloned.1.call-update) | async-done | bytes 16400
  697.9 44.4 %reduce-scatter.13.cloned.1.call-done = bf16[128,4096]{1,0:T(8,128)(2,1)} async-done(((bf16[512,4096]{1,0:T(8,128)(2,1)}), bf16[128,4096]{1,0:T(8,128)(2,1)}) %reduce-scatter.13.cloned.1.call-update) | async-done | bytes 1048592
  (138 shorter events, 50.6 us)
Async XLA Ops:
  7.2 1.0 copy-start
  7.2 40.2 %all-gather.2.cloned.1.call-start = ((), (), s32[]{:S(2)}) async-start(), calls=%async_computation.8 | async-start | bytes 5242880 | tf_op jit(solution)/shard_map/all_gather | solution.py:69
  8.1 20.9 %copy-start.20 = (bf16[512,128]{1,0:T(8,128)(2,1)S(1)}, bf16[512,128]{1,0:T(8,128)(2,1)}, u32[]{:S(2)}) copy-start(bf16[512,128]{1,0:T(8,128)(2,1)} %param.8) | copy-start | bytes 393220
  8.1 21.0 %copy-start.21 = (bf16[512,128]{1,0:T(8,128)(2,1)S(1)}, bf16[512,128]{1,0:T(8,128)(2,1)}, u32[]{:S(2)}) copy-start(bf16[512,128]{1,0:T(8,128)(2,1)} %param.9) | copy-start | bytes 393220
  29.0 0.8 copy-start.12
  29.8 22.1 %copy-start.13 = (bf16[512,128]{0,1:T(8,128)(2,1)}, bf16[512,128]{0,1:T(8,128)(2,1)S(1)}, u32[]{:S(2)}) copy-start(bf16[512,128]{0,1:T(8,128)(2,1)S(1)} %copy.58) | copy-start | bytes 393220
  29.8 27.5 %copy-start.22 = (bf16[2,3,3,128]{3,0,2,1:T(2,128)(2,1)S(1)}, bf16[2,3,3,128]{3,0,2,1:T(2,128)(2,1)}, u32[]{:S(2)}) copy-start(bf16[2,3,3,128]{3,0,2,1:T(2,128)(2,1)} %param.10) | copy-start | bytes 13828
  47.3 12.7 %slice-start = ((f32[1024,128]{1,0:T(8,128)}), f32[1,128]{1,0:T(1,128)S(1)}, s32[]{:S(2)}) async-start(f32[1024,128]{1,0:T(8,128)} %copy-done.12), calls=%async_computation.13 | async-start | bytes 1024 | tf_op jit(solution)/shard_map/slice | solution.py:32
  51.9 26.5 %collective-permute-start = (bf16[1,1024,256]{1,2,0:T(8,128)(2,1)}, bf16[1,1024,256]{1,2,0:T(8,128)(2,1)}, u32[]{:S(2)}, u32[]{:S(2)}) collective-permute-start(bf16[1,1024,256]{1,2,0:T(8,128)(2,1)} %get-tuple-element.50), channel_id=1, source_target_pairs={{0,4},{4,8},{8,12},{12,16},{16,20},{20,24},{24,28},{1,5},{5,9},{9,... | collective-permute-start | bytes 1572872 | tf_op jit(solution)/shard_map/ppermute | solution.py:18
  56.1 22.3 %collective-permute-start.1 = (bf16[1,1024,256]{1,2,0:T(8,128)(2,1)}, bf16[1,1024,256]{1,2,0:T(8,128)(2,1)}, u32[]{:S(2)}, u32[]{:S(2)}) collective-permute-start(bf16[1,1024,256]{1,2,0:T(8,128)(2,1)} %get-tuple-element.51), channel_id=1, source_target_pairs={{4,0},{8,4},{12,8},{16,12},{20,16},{24,20},{28,24},{5,1},{9,5},{13... | collective-permute-start | bytes 1572872 | tf_op jit(solution)/shard_map/ppermute | solution.py:19
  60.1 21.5 %copy-start.23 = (f32[1,1,256]{2,1,0:T(1,128)}, f32[1,1,256]{2,1,0:T(1,128)S(1)}, u32[]{:S(2)}) copy-start(f32[1,1,256]{2,1,0:T(1,128)S(1)} %get-tuple-element.62) | copy-start | bytes 3076
  60.1 21.5 %copy-start.25 = (f32[1,1,256]{2,1,0:T(1,128)}, f32[1,1,256]{2,1,0:T(1,128)S(1)}, u32[]{:S(2)}) copy-start(f32[1,1,256]{2,1,0:T(1,128)S(1)} %get-tuple-element.63) | copy-start | bytes 3076
  60.1 21.5 %copy-start.27 = (f32[1,1,256]{2,1,0:T(1,128)}, f32[1,1,256]{2,1,0:T(1,128)S(1)}, u32[]{:S(2)}) copy-start(f32[1,1,256]{2,1,0:T(1,128)S(1)} %get-tuple-element.64) | copy-start | bytes 3076
  60.1 21.5 %copy-start.29 = (f32[1,1,256]{2,1,0:T(1,128)}, f32[1,1,256]{2,1,0:T(1,128)S(1)}, u32[]{:S(2)}) copy-start(f32[1,1,256]{2,1,0:T(1,128)S(1)} %get-tuple-element.65) | copy-start | bytes 3076
  60.1 21.5 %copy-start.31 = (f32[1,1,256]{2,1,0:T(1,128)}, f32[1,1,256]{2,1,0:T(1,128)S(1)}, u32[]{:S(2)}) copy-start(f32[1,1,256]{2,1,0:T(1,128)S(1)} %get-tuple-element.66) | copy-start | bytes 3076
  81.6 7.7 %copy-start.2 = (f32[6,1026,256]{1,2,0:T(8,128)}, f32[6,1026,256]{1,2,0:T(8,128)S(1)}, u32[]{:S(2)}) copy-start(f32[6,1026,256]{1,2,0:T(8,128)S(1)} %fusion.22) | copy-start | bytes 18911236
  89.4 1.3 copy-start.10
  126.4 19.0 %copy-start.6 = (f32[4,1024,128]{2,1,0:T(8,128)}, f32[4,1024,128]{2,1,0:T(8,128)S(1)}, u32[]{:S(2)}) copy-start(f32[4,1024,128]{2,1,0:T(8,128)S(1)} %add_bitcast_fusion) | copy-start | bytes 6291460
  177.5 8.7 %copy-start.33 = (bf16[32,128]{1,0:T(8,128)(2,1)S(1)}, bf16[32,128]{1,0:T(8,128)(2,1)}, u32[]{:S(2)}) copy-start(bf16[32,128]{1,0:T(8,128)(2,1)} %param.12) | copy-start | bytes 24580
  179.3 55.2 %all-to-all-start = ((f32[4,1024,128]{2,0,1:T(4,128)}), f32[4,1024,128]{2,0,1:T(4,128)S(1)}, u32[]{:S(2)}, u32[]{:S(2)}) async-start(f32[4,1024,128]{2,0,1:T(4,128)} %copy.65), calls=%async_computation | async-start | bytes 4194304 | tf_op jit(solution)/shard_map/all_to_all | solution.py:108
  237.1 5.9 copy-start.4
  239.0 7.7 %copy-start.15 = (f32[1,128,128]{2,0,1:T(1,128)}, f32[1,128,128]{2,0,1:T(1,128)S(1)}, u32[]{:S(2)}) copy-start(f32[1,128,128]{2,0,1:T(1,128)S(1)} %slice.241) | copy-start | bytes 196612
  249.3 52.1 %all-to-all-start.1 = ((f32[32,128,128]{2,1,0:T(8,128)}), f32[32,128,128]{2,1,0:T(8,128)S(1)}, u32[]{:S(2)}, u32[]{:S(2)}) async-start(f32[32,128,128]{2,1,0:T(8,128)} %copy.67), calls=%async_computation.1 | async-start | bytes 4194304 | tf_op jit(solution)/shard_map/all_to_all | solution.py:110
  366.5 5.8 copy-start.5
  368.4 7.7 %copy-start.17 = (f32[1,128,128]{2,0,1:T(1,128)}, f32[1,128,128]{2,0,1:T(1,128)S(1)}, u32[]{:S(2)}) copy-start(f32[1,128,128]{2,0,1:T(1,128)S(1)} %slice.243) | copy-start | bytes 196612
  378.6 51.5 %all-to-all-start.3 = ((f32[32,128,128]{2,1,0:T(8,128)}), f32[32,128,128]{2,1,0:T(8,128)S(1)}, u32[]{:S(2)}, u32[]{:S(2)}) async-start(f32[32,128,128]{2,1,0:T(8,128)} %copy.72), calls=%async_computation.3 | async-start | bytes 4194304 | tf_op jit(solution)/shard_map/all_to_all | solution.py:115
  382.2 262.8 %reduce-scatter.11.cloned.1.call-start = ((), (), s32[]{:S(2)}) async-start(), calls=%async_computation.9 | async-start | bytes 294912 | tf_op jit(solution)/shard_map/reduce_scatter | solution.py:164
  430.1 2.2 copy-start.9
  439.1 2.1 copy-start.8
  439.1 19.3 %copy-start.7 = (f32[4,1024,128]{2,1,0:T(8,128)S(1)}, f32[4,1024,128]{2,1,0:T(8,128)}, u32[]{:S(2)}) copy-start(f32[4,1024,128]{2,1,0:T(8,128)} %copy-done.6) | copy-start | bytes 6291460
  475.4 1.6 copy-start.3
  475.6 7.7 %copy-start.19 = (f32[1024,128]{1,0:T(8,128)S(1)}, f32[1024,128]{1,0:T(8,128)}, u32[]{:S(2)}) copy-start(f32[1024,128]{1,0:T(8,128)} %get-tuple-element.43) | copy-start | bytes 1572868
  478.6 48.2 %collective-permute-start.2 = (f32[1,1024,256]{1,2,0:T(8,128)}, f32[1,1024,256]{1,2,0:T(8,128)S(1)}, u32[]{:S(2)}, u32[]{:S(2)}) collective-permute-start(f32[1,1024,256]{1,2,0:T(8,128)} %get-tuple-element.45), channel_id=1, source_target_pairs={{0,4},{4,8},{8,12},{12,16},{16,20},{20,24},{24,28},{1,5},{5,9},{9,... | collective-permute-start | bytes 3145736 | tf_op jit(solution)/shard_map/ppermute | solution.py:18
  482.0 44.8 %collective-permute-start.3 = (f32[1,1024,256]{1,2,0:T(8,128)}, f32[1,1024,256]{1,2,0:T(8,128)}, u32[]{:S(2)}, u32[]{:S(2)}) collective-permute-start(f32[1,1024,256]{1,2,0:T(8,128)} %get-tuple-element.46), channel_id=1, source_target_pairs={{4,0},{8,4},{12,8},{16,12},{20,16},{24,20},{28,24},{5,1},{9,5},{13... | collective-permute-start | bytes 3145736 | tf_op jit(solution)/shard_map/ppermute | solution.py:19
  508.3 27.2 %copy-start.24 = (f32[1,1,256]{2,1,0:T(1,128)S(1)}, f32[1,1,256]{2,1,0:T(1,128)}, u32[]{:S(2)}) copy-start(f32[1,1,256]{2,1,0:T(1,128)} %copy-done.23) | copy-start | bytes 3076
  508.3 27.2 %copy-start.26 = (f32[1,1,256]{2,1,0:T(1,128)S(1)}, f32[1,1,256]{2,1,0:T(1,128)}, u32[]{:S(2)}) copy-start(f32[1,1,256]{2,1,0:T(1,128)} %copy-done.25) | copy-start | bytes 3076
  508.4 27.2 %copy-start.28 = (f32[1,1,256]{2,1,0:T(1,128)S(1)}, f32[1,1,256]{2,1,0:T(1,128)}, u32[]{:S(2)}) copy-start(f32[1,1,256]{2,1,0:T(1,128)} %copy-done.27) | copy-start | bytes 3076
  508.4 27.2 %copy-start.30 = (f32[1,1,256]{2,1,0:T(1,128)S(1)}, f32[1,1,256]{2,1,0:T(1,128)}, u32[]{:S(2)}) copy-start(f32[1,1,256]{2,1,0:T(1,128)} %copy-done.29) | copy-start | bytes 3076
  508.4 27.2 %copy-start.32 = (f32[1,1,256]{2,1,0:T(1,128)S(1)}, f32[1,1,256]{2,1,0:T(1,128)}, u32[]{:S(2)}) copy-start(f32[1,1,256]{2,1,0:T(1,128)} %copy-done.31) | copy-start | bytes 3076
  508.4 138.0 %reduce-scatter.15.cloned.1.call-start = ((), (), s32[]{:S(2)}) async-start(), calls=%async_computation.11 | async-start | bytes 147456
  551.1 5.8 copy-start.14
  556.1 140.3 %reduce-scatter.17.cloned.1.call-start = ((), (), s32[]{:S(2)}) async-start(), calls=%async_computation.12 | async-start | bytes 147456
  556.9 185.4 %reduce-scatter.13.cloned.1.call-start = ((), (), s32[]{:S(2)}) async-start(), calls=%async_computation.10 | async-start | bytes 5242880
  576.5 0.7 copy-start.34
  576.5 1.9 copy-start.11
  576.5 3.2 copy-start.16
  576.5 3.2 copy-start.18
  606.6 139.3 %copy-start.1 = (bf16[1024,128]{1,0:T(8,128)(2,1)S(1)}, bf16[1024,128]{1,0:T(8,128)(2,1)}, u32[]{:S(2)}) copy-start(bf16[1024,128]{1,0:T(8,128)(2,1)} %param.11) | copy-start | bytes 786436
Sparse Core Ops, SparseCore 0:
  9.6 37.7 all-gather.1
  508.5 61.5 reduce-scatter.10
  573.4 59.8 reduce-scatter.14
  636.4 59.8 reduce-scatter.16
  698.7 43.5 reduce-scatter.12
where the time goes:
time: 763 us; the launch traced here: 753 us
  waiting for transfers between devices  253 us (33%)
  matrix products  152 us (20%)
  other arithmetic  113 us (15%)
  local copies, waits for them, and re-layouts  103 us (13%)
  blocking collectives  92.2 us (12%)
  starting transfers between devices  24.4 us (3%)
  between operations  15.7 us (2%)
    unnamed x8, waiting for transfers between devices  93.5 us
    all_to_all x1, blocking collectives, local(): lax.all_to_all(grad_mix, 'grid', split_axis=1, concat_axis=0, tiled=True)  52.3 us
    all_to_all x1, waiting for transfers between devices, local(): lax.all_to_all(mix_row, 'grid', split_axis=1, concat_axis=0, tiled=True)  48.1 us
    all_to_all x1, waiting for transfers between devices, local(): lax.all_to_all(mixed_cols, 'grid', split_axis=0, concat_axis=1, tiled=True)  46.2 us
    rev x6, local copies, waits for them, and re-layouts, mirror(): return jnp.concatenate([leading, jnp.flip(remainder, along)], axis=along)  45.1 us
    ppermute x2, waiting for transfers between devices, extended(): before = lax.ppermute(last, axis, up)  35.3 us
    unnamed x87, local copies, waits for them, and re-layouts  34 us
    dot_general x1, matrix products, local(): jnp.einsum('rkc,kw->rwc', row_mixed, cas_width, precision=highest)  30.1 us
  transfers between devices with their start and end apart: 12, of which 8 were waited for; matrix products, arithmetic and copies ran while one was open for 22% of the time, Pallas kernels for 0%

commit v1 on v0

v1 whole, which is shorter than its diff:
```python
import math

import jax
import jax.numpy as jnp
import ml_dtypes
import numpy as np
from jax import lax
from jax.sharding import PartitionSpec as P

bf16 = jnp.bfloat16
f32 = jnp.float32


def basis(length, tiles):
    half = length // 2
    per = half // tiles
    position = np.arange(length)
    columns, weights = [], []
    for tile in range(tiles):
        freqs = np.arange(tile * per, (tile + 1) * per)
        phase = (position[:, None] * freqs[None, :] % length) * (2.0 * math.pi / length)
        sines = np.sin(phase)
        weight = np.full((2 * per,), 2.0 / length)
        if tile == 0:
            sines[:, 0] = np.where(position % 2 == 0, 1.0, -1.0)
            weight[0] = weight[per] = 1.0 / length
        columns += [np.cos(phase), sines]
        weights.append(weight)
    return np.concatenate(columns, axis=1), np.concatenate(weights)


def parts(spectrum, axis):
    return jnp.split(spectrum, 2, axis=axis)


def filter_parts(spectrum, first):
    cos, sin = parts(spectrum, 0)
    row = lax.broadcasted_iota(jnp.int32, cos.shape, 0) == 0
    packed = jnp.logical_and(row, first)
    return cos, jnp.where(packed, 0.0, sin), jnp.where(packed, sin, cos)


def times(spectrum, coef, axis):
    x, y = parts(spectrum, axis)
    p, q, p2 = coef
    return jnp.concatenate([x * p - y * q, x * q + y * p2], axis=axis)


def times_conj(spectrum, coef, axis):
    x, y = parts(spectrum, axis)
    p, q, p2 = coef
    return jnp.concatenate([x * p + y * q, y * p2 - x * q], axis=axis)


def correlate(a, b, axis, total, first):
    ax, ay = parts(a, axis)
    bx, by = parts(b, axis)
    xx, yy = jnp.sum(ax * bx, axis=total), jnp.sum(ay * by, axis=total)
    cross = jnp.sum(ay * bx - ax * by, axis=total)
    row = lax.broadcasted_iota(jnp.int32, xx.shape, 0) == 0
    packed = jnp.logical_and(row, first)
    return jnp.concatenate(
        [jnp.where(packed, xx, xx + yy), jnp.where(packed, yy, cross)], axis=0
    )


def dot(spec, a, b):
    return jnp.einsum(spec, a.astype(bf16), b.astype(bf16), preferred_element_type=f32)


def halo(value):
    size = lax.axis_size("grid")
    up = [(i, i + 1) for i in range(size - 1)]
    down = [(i + 1, i) for i in range(size - 1)]
    before = lax.ppermute(value[-1:], "grid", up)
    after = lax.ppermute(value[:1], "grid", down)
    return jnp.concatenate([before, value, after], axis=0)


def local(inputs, w_gate, w_value, short_filter, row_filter, column_filter, cotangent):
    tile_rows, width, channels = inputs.shape
    height = column_filter.shape[0]
    tiles = lax.axis_size("grid")
    me = lax.axis_index("grid")
    first = me == 0
    per = width // tiles
    scale = 1.0 / math.sqrt(height * width)

    wide, wide_weight = basis(width, tiles)
    tall, tall_weight = basis(height, 1)
    wide = jnp.asarray(wide.astype(ml_dtypes.bfloat16))
    tall = jnp.asarray(tall.astype(ml_dtypes.bfloat16))
    tall_weight = jnp.asarray(tall_weight, f32)[:, None]
    wide_weight = lax.dynamic_slice_in_dim(jnp.asarray(wide_weight, f32), me * per, per, 0)[:, None]
    wide_own = lax.dynamic_slice_in_dim(wide, me * per, per, 1)

    gathered = lax.all_gather(inputs, "ch", axis=2, tiled=True)
    w_both = jnp.concatenate([w_gate, w_value], axis=1)
    kernel = jnp.concatenate([short_filter[0], short_filter[1]], axis=-1).astype(f32)
    row_coef = filter_parts(dot("mk,mc->kc", wide_own, row_filter), first)
    col_coef = filter_parts(dot("mk,mc->kc", tall, column_filter), True)
    col_coef = tuple(v[:, None, :] for v in col_coef)

    stacked = dot("rwd,dc->rwc", gathered, w_both).astype(bf16)
    framed = jnp.pad(halo(stacked), ((0, 0), (1, 1), (0, 0)))
    featured = jnp.zeros((tile_rows, width, 2 * channels), f32)
    for i in range(3):
        for j in range(3):
            featured = featured + kernel[i, j] * framed[i : i + tile_rows, j : j + width].astype(f32)
    featured = featured.astype(bf16)
    gate_feat = featured[..., :channels].astype(f32)
    value_bf = featured[..., channels:]
    grad_out = cotangent.astype(f32)
    grad_mix = (grad_out * gate_feat).astype(bf16)

    def to_columns(field):
        spectrum = dot("wk,rwc->rkc", wide, field).astype(bf16)
        return lax.all_to_all(spectrum, "grid", split_axis=1, concat_axis=0, tiled=True).astype(f32)

    def to_rows(spectrum):
        spectrum = (spectrum * wide_weight).astype(bf16)
        back = lax.all_to_all(spectrum, "grid", split_axis=0, concat_axis=1, tiled=True)
        return dot("wk,rkc->rwc", wide, back)

    value_spec = to_columns(value_bf)
    grad_spec = to_columns(grad_mix)

    mixed_rows = times(value_spec, row_coef, 1)
    value_tall = dot("hk,hwc->kwc", tall, mixed_rows)
    mixed = dot("hk,kwc->hwc", tall, times(value_tall, col_coef, 0) * tall_weight[:, None])
    mix_col = to_rows(mixed)

    grad_tall = dot("hk,hwc->kwc", tall, grad_spec)
    grad_row = dot("hk,kwc->hwc", tall, times_conj(grad_tall, col_coef, 0) * tall_weight[:, None])
    grad_value = to_rows(times_conj(grad_row, row_coef, 1))

    col_term = correlate(grad_tall * wide_weight, value_tall, 0, 1, True)
    col_grad = dot("mk,kc->mc", tall, col_term * tall_weight) * scale
    row_term = correlate(grad_row, value_spec, 1, 0, first)
    row_grad = dot("mk,kc->mc", wide_own, row_term * wide_weight) * scale

    gated = (gate_feat * mix_col).astype(bf16)
    grad_gate = grad_out * mix_col
    grad_feat = jnp.concatenate([grad_gate, grad_value], axis=2).astype(bf16)
    grad_framed = jnp.pad(halo(grad_feat), ((0, 0), (1, 1), (0, 0)))
    back_sum = jnp.zeros((tile_rows, width, 2 * channels), f32)
    short_rows = []
    for i in range(3):
        for j in range(3):
            back_sum = back_sum + kernel[i, j] * grad_framed[
                2 - i : 2 - i + tile_rows, 2 - j : 2 - j + width
            ].astype(f32)
            short_rows.append(
                jnp.sum(
                    grad_feat.astype(f32) * framed[i : i + tile_rows, j : j + width].astype(f32),
                    axis=(0, 1),
                )
            )
    back_stack = back_sum.astype(bf16)
    partial_term = dot("rwc,dc->rwd", back_stack, w_both).astype(bf16)
    partial_term = partial_term.reshape(tile_rows, width, lax.axis_size("ch"), channels)
    input_grad = lax.psum_scatter(
        partial_term.reshape(tile_rows, width, -1), "ch", scatter_dimension=2, tiled=True
    )

    weight_term = dot("rwd,rwc->dc", gathered, back_stack) * scale
    short_term = jnp.stack(short_rows).reshape(9, 2 * channels) * scale
    short_term = jnp.concatenate([short_term[:, :channels], short_term[:, channels:]], axis=0)
    depth = weight_term.shape[0]

    def cut(term):
        return term.reshape(tiles, term.shape[0] // tiles, channels)

    packed = jnp.concatenate(
        [
            cut(weight_term[:, :channels]),
            cut(weight_term[:, channels:]),
            cut(row_grad),
            cut(col_grad),
            jnp.broadcast_to(short_term[None], (tiles, 18, channels)),
        ],
        axis=1,
    ).astype(bf16)
    arrived = lax.all_to_all(packed, "grid", split_axis=0, concat_axis=0, tiled=True)
    total = jnp.sum(arrived.astype(f32), axis=0)
    ends = np.cumsum([depth // tiles, depth // tiles, per, height // tiles])
    gate_grad, value_grad, row_share, col_share, short_sum = jnp.split(total, ends, axis=0)
    return (
        gated,
        input_grad,
        gate_grad,
        value_grad,
        short_sum.reshape(2, 3, 3, channels),
        row_share,
        col_share,
    )


def solution(mesh):
    return jax.shard_map(
        local,
        mesh=mesh,
        in_specs=(
            P("grid", None, "ch"),
            P(None, "ch"),
            P(None, "ch"),
            P(None, None, None, "ch"),
            P(None, "ch"),
            P(None, "ch"),
            P("grid", None, "ch"),
        ),
        out_specs=(
            P("grid", None, "ch"),
            P("grid", None, "ch"),
            P("grid", "ch"),
            P("grid", "ch"),
            P(None, None, None, "ch"),
            P("grid", "ch"),
            P("grid", "ch"),
        ),
        check_vma=False,
    )
```

time: 763 us -> 343 us (0.45); the launches traced: 753 us -> 342 us
  matrix products: 152 us -> 30.5 us
  blocking collectives: 92.2 us -> 0 us
  other arithmetic: 113 us -> 38.2 us
  waiting for transfers between devices: 253 us -> 179 us
  local copies, waits for them, and re-layouts: 103 us -> 46 us
  starting transfers between devices: 24.4 us -> 33.1 us
    dot_general x15, matrix products: 143 us -> 30.5 us  [dot(): jnp.einsum(spec, a.astype(bf16), b.astype(bf16), preferred_element_type=f32)]
    unnamed x8 -> x3, waiting for transfers between devices: 93.5 us -> 0.7 us
    all_to_all x1 -> x0, blocking collectives: 52.3 us -> none  [local(): lax.all_to_all(grad_mix, 'grid', split_axis=1, concat_axis=0, tiled=True)]
    rev x6 -> x0, local copies, waits for them, and re-layouts: 45.1 us -> none  [mirror(): return jnp.concatenate([leading, jnp.flip(remainder, along)], axis=along)]
    unnamed x1 -> x0, blocking collectives: 21.7 us -> none
    all_gather x1, waiting for transfers between devices: 17.5 us -> 37.4 us  [local(): gathered = lax.all_gather(inputs, 'ch', axis=2, tiled=True)]
    dot_general x2 -> x0, other arithmetic: 19.7 us -> none  [the longest x1 17.7 us: local(): spec_gr = jnp.einsum('rwc,wk->rkc', grad_row, cas_width, precision=highest)]
    psum x1 -> x0, blocking collectives: 18.3 us -> none  [local(): short_grad = lax.psum(short_term, 'grid')]
  transfers between devices with their start and end apart: 12 -> 11, of which waited for: 8 -> 8; matrix products, arithmetic and copies ran while one was open for 22% -> 14% of each run, Pallas kernels for 0% -> 0%
where the time goes in v1:
time: 343 us; the launch traced here: 342 us
  waiting for transfers between devices  179 us (52%)
  local copies, waits for them, and re-layouts  46 us (13%)
  other arithmetic  38.2 us (11%)
  starting transfers between devices  33.1 us (10%)
  matrix products  30.5 us (9%)
  between operations  14.9 us (4%)
    all_to_all x2, waiting for transfers between devices, to_rows(): lax.all_to_all(spectrum, 'grid', split_axis=0, concat_axis=1, tiled=True)  43.4 us
    all_to_all x2, waiting for transfers between devices, to_columns(): lax.all_to_all(spectrum, 'grid', split_axis=1, concat_axis=0, tiled=True)  41.9 us
    ppermute x2, waiting for transfers between devices, halo(): before = lax.ppermute(value[-1:], 'grid', up)  41.4 us
    all_gather x1, waiting for transfers between devices, local(): gathered = lax.all_gather(inputs, 'ch', axis=2, tiled=True)  37.4 us
    dot_general x15, matrix products, dot(): jnp.einsum(spec, a.astype(bf16), b.astype(bf16), preferred_element_type=f32)  30.5 us
    unnamed x89, local copies, waits for them, and re-layouts  26.6 us
    all_to_all x1, waiting for transfers between devices, local(): lax.all_to_all(packed, 'grid', split_axis=0, concat_axis=0, tiled=True)  14.4 us
    all_to_all x2, starting transfers between devices, to_columns(): lax.all_to_all(spectrum, 'grid', split_axis=1, concat_axis=0, tiled=True)  10.9 us
  transfers between devices with their start and end apart: 11, of which 8 were waited for; matrix products, arithmetic and copies ran while one was open for 14% of the time, Pallas kernels for 0%

profile of v1, /device:TPU:0, one launch (start us, length us, event | category | flops | bytes accessed | tf_op | source)
XLA Modules:
  0.0 341.9 jit_solution(14000975871945595255)
XLA Ops:
  10.0 37.4 %all-gather.2.cloned.1.call-done = bf16[4,1024,512]{2,1,0:T(8,128)(2,1)} async-done(((bf16[4,1024,128]{2,1,0:T(8,128)(2,1)}), bf16[4,1024,512]{2,1,0:T(8,128)(2,1)}) %all-gather.2.cloned.1.call-update) | async-done | bytes 4194320 | tf_op jit(solution)/shard_map/all_gather | solution.py:97
  47.3 3.5 %convert_bitcast_fusion = bf16[4,1024,256]{1,2,0:T(8,128)(2,1)S(1)} fusion(bf16[4,1024,512]{2,1,0:T(8,128)(2,1)} %all-gather.2.cloned.1.call-done, bf16[512,128]{0,1:T(8,128)(2,1)S(1)} %copy.51, bf16[512,128]{0,1:T(8,128)(2,1)S(1)} %copy.50), kind=kOutput, calls=%fused_computation.77 | convolution fusion | flops 1075314688 | bytes 6553600 | tf_op jit(solution)/shard_map/rwd,dc->rwc/dot_general | solution.py:68
  50.9 3.4 collective-permute-start
  54.3 1.3 collective-permute-start.1
  55.8 21.3 %collective-permute-done = bf16[1,1024,256]{1,2,0:T(8,128)(2,1)S(1)} collective-permute-done((bf16[1,1024,256]{1,2,0:T(8,128)(2,1)S(1)}, bf16[1,1024,256]{1,2,0:T(8,128)(2,1)S(1)}, u32[]{:S(2)}, u32[]{:S(2)}) %collective-permute-start) | collective-permute-done | bytes 524320 | tf_op jit(solution)/shard_map/ppermute | solution.py:75
  77.1 2.5 select_maximum_fusion.3
  79.6 6.9 %fusion.9 = bf16[4,1024,256]{1,2,0:T(8,128)(2,1)S(1)} fusion(bf16[4,1024,256]{1,2,0:T(8,128)(2,1)S(1)} %convert_bitcast_fusion, bf16[1,1024,256]{1,2,0:T(8,128)(2,1)S(1)} %collective-permute-done.1, bf16[1,1024,256]{1,2,0:T(8,128)(2,1)S(1)} %collective-permute-done, f32[256]{0:T(256)S(1)} %bitcast.134, f32[256]{0:T(256)S(1)} %bitcast.120, ...), kind=kLoop, calls=%fused_computation.30 | loop fusion | flops 30408704 | bytes 17835008 | tf_op jit(solution)/shard_map/convert_element_type | solution.py:110
  86.6 1.3 copy-done.10
  87.9 1.3 fusion.32
  89.2 1.4 copy.52
  90.7 6.5 %all-to-all-start = ((bf16[4,1024,128]{2,0,1:T(4,128)(2,1)}), bf16[4,1024,128]{2,0,1:T(4,128)(2,1)S(1)}, u32[]{:S(2)}, u32[]{:S(2)}) async-start(bf16[4,1024,128]{2,0,1:T(4,128)(2,1)} %copy.52), calls=%async_computation | async-start | bytes 2097152 | tf_op jit(solution)/shard_map/all_to_all | solution.py:118
  97.2 1.3 copy.57
  98.5 3.5 %fusion.33 = bf16[4,1024,128]{1,2,0:T(8,128)(2,1)S(1)} fusion(bf16[1024,1024,1]{1,0,2:T(8,128)(2,1)} %constant.45, bf16[4,1024,128]{1,2,0:T(8,128)(2,1)} %copy.57, bf16[4,1024,256]{1,2,0:T(8,128)(2,1)} %copy-done.10), kind=kOutput, calls=%fused_computation.82 | convolution fusion | flops 1076363264 | bytes 5242880 | tf_op jit(solution)/shard_map/wk,rwc->rkc/dot_general | solution.py:68
  102.0 1.4 copy.58
  103.4 19.7 %all-to-all-done = bf16[4,1024,128]{2,0,1:T(4,128)(2,1)S(1)} async-done(((bf16[4,1024,128]{2,0,1:T(4,128)(2,1)}), bf16[4,1024,128]{2,0,1:T(4,128)(2,1)S(1)}, u32[]{:S(2)}, u32[]{:S(2)}) %all-to-all-start) | async-done | bytes 1048608 | tf_op jit(solution)/shard_map/all_to_all | solution.py:118
  123.1 4.4 %all-to-all-start.2 = ((bf16[4,1024,128]{2,0,1:T(4,128)(2,1)}), bf16[4,1024,128]{2,0,1:T(4,128)(2,1)}, u32[]{:S(2)}, u32[]{:S(2)}) async-start(bf16[4,1024,128]{2,0,1:T(4,128)(2,1)} %copy.58), calls=%async_computation.2 | async-start | bytes 2097152 | tf_op jit(solution)/shard_map/all_to_all | solution.py:118
  129.0 1.2 fusion.58
  130.8 22.2 %all-to-all-done.2 = bf16[4,1024,128]{2,0,1:T(4,128)(2,1)} async-done(((bf16[4,1024,128]{2,0,1:T(4,128)(2,1)}), bf16[4,1024,128]{2,0,1:T(4,128)(2,1)}, u32[]{:S(2)}, u32[]{:S(2)}) %all-to-all-start.2) | async-done | bytes 1048608 | tf_op jit(solution)/shard_map/all_to_all | solution.py:118
  153.0 1.4 copy.59
  155.9 1.8 multiply_reduce_fusion.3
  160.1 1.4 copy.55
  161.5 3.6 %all-to-all-start.1 = ((bf16[32,128,128]{2,1,0:T(8,128)(2,1)}), bf16[32,128,128]{2,1,0:T(8,128)(2,1)S(1)}, u32[]{:S(2)}, u32[]{:S(2)}) async-start(bf16[32,128,128]{2,1,0:T(8,128)(2,1)} %copy.55), calls=%async_computation.1 | async-start | bytes 2097152 | tf_op jit(solution)/shard_map/all_to_all | solution.py:122
  165.0 1.4 copy.62
  166.4 24.3 %all-to-all-done.1 = bf16[32,128,128]{2,1,0:T(8,128)(2,1)S(1)} async-done(((bf16[32,128,128]{2,1,0:T(8,128)(2,1)}), bf16[32,128,128]{2,1,0:T(8,128)(2,1)S(1)}, u32[]{:S(2)}, u32[]{:S(2)}) %all-to-all-start.1) | async-done | bytes 1048608 | tf_op jit(solution)/shard_map/all_to_all | solution.py:122
  190.8 3.6 %all-to-all-start.3 = ((bf16[32,128,128]{2,1,0:T(8,128)(2,1)}), bf16[32,128,128]{2,1,0:T(8,128)(2,1)S(1)}, u32[]{:S(2)}, u32[]{:S(2)}) async-start(bf16[32,128,128]{2,1,0:T(8,128)(2,1)} %copy.62), calls=%async_computation.3 | async-start | bytes 2097152 | tf_op jit(solution)/shard_map/all_to_all | solution.py:122
  195.2 1.3 all_to_all.53
  196.4 4.8 %fusion.27 = (bf16[4,1024,128]{1,2,0:T(8,128)(2,1)S(1)}, bf16[4,1024,128]{1,2,0:T(8,128)(2,1)}) fusion(bf16[4,1024,128]{1,2,0:T(8,128)(2,1)} %copy.57, bf16[4,1024,256]{1,2,0:T(8,128)(2,1)} %copy-done.10, bf16[4,1024,128]{1,2,0:T(8,128)(2,1)} %all_to_all.53, bf16[1024,1024,1]{1,0,2:T(8,128)(2,1)} %constant.45), kind=kOutput, calls=%fused_computation.62 | convolution fusion | flops 1076887552 | bytes 7340032 | tf_op jit(solution)/shard_map/wk,rkc->rwc/dot_general | solution.py:68
  201.3 19.1 %all-to-all-done.3 = bf16[32,128,128]{2,1,0:T(8,128)(2,1)S(1)} async-done(((bf16[32,128,128]{2,1,0:T(8,128)(2,1)}), bf16[32,128,128]{2,1,0:T(8,128)(2,1)S(1)}, u32[]{:S(2)}, u32[]{:S(2)}) %all-to-all-start.3) | async-done | bytes 1048608 | tf_op jit(solution)/shard_map/all_to_all | solution.py:122
  221.6 2.9 fusion.34
  224.6 3.5 %collective-permute-start.2 = (bf16[1,1024,256]{1,2,0:T(8,128)(2,1)S(1)}, bf16[1,1024,256]{1,2,0:T(8,128)(2,1)S(1)}, u32[]{:S(2)}, u32[]{:S(2)}) collective-permute-start(bf16[1,1024,256]{1,2,0:T(8,128)(2,1)S(1)} %get-tuple-element.63), channel_id=1, source_target_pairs={{0,4},{4,8},{8,12},{12,16},{16,20},{20,24},{24,28},{1,5},{5,9},{9,... | collective-permute-start | bytes 1572872 | tf_op jit(solution)/shard_map/ppermute | solution.py:75
  228.1 1.5 collective-permute-start.3
  229.6 20.1 %collective-permute-done.2 = bf16[1,1024,256]{1,2,0:T(8,128)(2,1)S(1)} collective-permute-done((bf16[1,1024,256]{1,2,0:T(8,128)(2,1)S(1)}, bf16[1,1024,256]{1,2,0:T(8,128)(2,1)S(1)}, u32[]{:S(2)}, u32[]{:S(2)}) %collective-permute-start.2) | collective-permute-done | bytes 524320 | tf_op jit(solution)/shard_map/ppermute | solution.py:75
  249.7 3.8 %select_maximum_fusion = bf16[6,1026,256]{1,2,0:T(8,128)(2,1)S(1)} fusion(bf16[1,1024,256]{1,2,0:T(8,128)(2,1)S(1)} %collective-permute-done.3, bf16[1,1024,256]{1,2,0:T(8,128)(2,1)S(1)} %collective-permute-done.2, bf16[4,1024,128]{1,2,0:T(8,128)(2,1)S(1)} %fusion.34, bf16[4,1024,128]{1,2,0:T(8,128)(2,1)S(1)} %get-tuple-element.65), kind=kLoop, calls=%fused_computation.46 | loop fusion | flops 23639040 | bytes 6297600 | tf_op jit(solution)/shard_map/concatenate | solution.py:77
  253.6 8.7 %fusion.15 = bf16[4,1024,256]{1,2,0:T(8,128)(2,1)S(1)} fusion(bf16[6,1026,256]{1,2,0:T(8,128)(2,1)S(1)} %select_maximum_fusion, bf16[1,1024,256]{1,2,0:T(8,128)(2,1)S(1)} %collective-permute-done.2, bf16[4,1024,128]{1,2,0:T(8,128)(2,1)S(1)} %fusion.34, bf16[4,1024,128]{1,2,0:T(8,128)(2,1)S(1)} %get-tuple-element.65, ...), kind=kLoop, calls=%fused_computation.36 | loop fusion | flops 41943040 | bytes 17835008 | tf_op jit(solution)/shard_map/convert_element_type | solution.py:159
  262.3 1.3 copy-done.7
  263.7 3.3 convolution_convert_fusion
  267.0 8.1 %copy.77 = bf16[4,1024,512]{1,0,2:T(4,128)(2,1)} copy(bf16[4,1024,512]{2,1,0:T(8,128)(2,1)} %convolution_convert_fusion) | data formatting | bytes 8388608
  275.1 6.5 %copy.81 = bf16[64,8,4,1024]{3,1,2,0:T(8,128)(2,1)} copy(bf16[64,8,4,1024]{3,2,1,0:T(4,128)(2,1)} %bitcast.104) | data formatting | bytes 8388608
  284.5 2.0 fusion.38
  286.4 10.8 %fusion.23 = (f32[256]{0:T(256)S(1)}, f32[256]{0:T(256)S(1)}, f32[256]{0:T(256)}, f32[256]{0:T(256)}, f32[256]{0:T(256)}, /*index=5*/f32[256]{0:T(256)}, f32[256]{0:T(256)}, f32[256]{0:T(256)}, f32[256]{0:T(256)}) fusion(bf16[1,1024,256]{1,2,0:T(8,128)(2,1)} %copy-done.9, bf16[4,1024,256]{1,2,0:T(8,128)(2,1)} %copy-done.4, ...), kind=kLoop, calls=%fused_computation.44 | loop fusion | flops 38795008 | bytes 17835008 | tf_op jit(solution)/shard_map/reduce_sum | solution.py:154
  297.2 1.4 stack.39
  298.7 4.8 %fusion.39 = bf16[512,256]{0,1:T(8,128)(2,1)S(1)} fusion(bf16[4,1024,256]{1,2,0:T(8,128)(2,1)} %copy-done.7, bf16[4,1024,512]{2,1,0:T(8,128)(2,1)} %all-gather.2.cloned.1.call-done), kind=kOutput, calls=%fused_computation.90 | convolution fusion | flops 1074003968 | bytes 6553600 | tf_op jit(solution)/shard_map/rwd,rwc->dc/dot_general | solution.py:68
  303.8 4.2 %concatenate.70 = bf16[8,278,128]{2,1,0:T(8,128)(2,1)} concatenate(bf16[8,64,128]{2,1,0:T(8,128)(2,1)S(1)} %bitcast.114, bf16[8,64,128]{2,1,0:T(8,128)(2,1)S(1)} %bitcast.115, bf16[8,128,128]{2,1,0:T(8,128)(2,1)S(1)} %bitcast.113, bf16[8,4,128]{2,1,0:T(4,128)(2,1)S(1)} %bitcast.136, bf16[8,18,128]{2,1,0:T(8,128)(2,1)S(1)} %broadcast_in_dim.12), dimensions={1} | concatenate | bytes 1138688 | tf_op jit(solution)/shard_map/concatenate | solution.py:174
  308.0 5.2 %all-to-all-start.4 = ((bf16[8,278,128]{2,1,0:T(8,128)(2,1)}), bf16[8,278,128]{2,1,0:T(8,128)(2,1)S(1)}, u32[]{:S(2)}, u32[]{:S(2)}) async-start(bf16[8,278,128]{2,1,0:T(8,128)(2,1)} %concatenate.70), calls=%async_computation.4 | async-start | bytes 1146880 | tf_op jit(solution)/shard_map/all_to_all | solution.py:184
  313.2 1.3 copy.68
  314.5 14.4 %all-to-all-done.4 = bf16[8,278,128]{2,1,0:T(8,128)(2,1)S(1)} async-done(((bf16[8,278,128]{2,1,0:T(8,128)(2,1)}), bf16[8,278,128]{2,1,0:T(8,128)(2,1)S(1)}, u32[]{:S(2)}, u32[]{:S(2)}) %all-to-all-start.4) | async-done | bytes 569376 | tf_op jit(solution)/shard_map/all_to_all | solution.py:184
  331.5 1.8 reshape.68
  333.4 1.7 copy.78
  (125 shorter events, 16.5 us)
Async XLA Ops:
  7.2 121.8 %copy-start = (bf16[1024,128]{1,0:T(8,128)(2,1)S(1)}, bf16[1024,128]{1,0:T(8,128)(2,1)}, u32[]{:S(2)}) copy-start(bf16[1024,128]{1,0:T(8,128)(2,1)} %param.15) | copy-start | bytes 786436
  7.2 40.1 %all-gather.2.cloned.1.call-start = ((), (), s32[]{:S(2)}) async-start(), calls=%async_computation.6 | async-start | bytes 5242880 | tf_op jit(solution)/shard_map/all_gather | solution.py:97
  9.9 45.7 %copy-start.15 = (bf16[2,3,3,128]{3,0,2,1:T(2,128)(2,1)S(1)}, bf16[2,3,3,128]{3,0,2,1:T(2,128)(2,1)}, u32[]{:S(2)}) copy-start(bf16[2,3,3,128]{3,0,2,1:T(2,128)(2,1)} %param.14) | copy-start | bytes 13828
  50.8 35.7 %copy-start.4 = (bf16[4,1024,256]{1,2,0:T(8,128)(2,1)}, bf16[4,1024,256]{1,2,0:T(8,128)(2,1)S(1)}, u32[]{:S(2)}) copy-start(bf16[4,1024,256]{1,2,0:T(8,128)(2,1)S(1)} %convert_bitcast_fusion) | copy-start | bytes 6291460
  50.9 26.2 %collective-permute-start = (bf16[1,1024,256]{1,2,0:T(8,128)(2,1)S(1)}, bf16[1,1024,256]{1,2,0:T(8,128)(2,1)S(1)}, u32[]{:S(2)}, u32[]{:S(2)}) collective-permute-start(bf16[1,1024,256]{1,2,0:T(8,128)(2,1)S(1)} %get-tuple-element.67), channel_id=1, source_target_pairs={{0,4},{4,8},{8,12},{12,16},{16,20},{20,24},{24,28},{1,5},{5,9},{9,... | collective-permute-start | bytes 1572872 | tf_op jit(solution)/shard_map/ppermute | solution.py:75
  54.3 22.8 %collective-permute-start.1 = (bf16[1,1024,256]{1,2,0:T(8,128)(2,1)S(1)}, bf16[1,1024,256]{1,2,0:T(8,128)(2,1)S(1)}, u32[]{:S(2)}, u32[]{:S(2)}) collective-permute-start(bf16[1,1024,256]{1,2,0:T(8,128)(2,1)S(1)} %get-tuple-element.68), channel_id=1, source_target_pairs={{4,0},{8,4},{12,8},{16,12},{20,16},{24,20},{28,24},{5,1},{9,5},{13... | collective-permute-start | bytes 1572872 | tf_op jit(solution)/shard_map/ppermute | solution.py:76
  55.7 30.8 %copy-start.16 = (f32[1,1,256]{2,1,0:T(1,128)}, f32[1,1,256]{2,1,0:T(1,128)S(1)}, u32[]{:S(2)}) copy-start(f32[1,1,256]{2,1,0:T(1,128)S(1)} %get-tuple-element.87) | copy-start | bytes 3076
  55.7 30.8 %copy-start.18 = (f32[1,1,256]{2,1,0:T(1,128)}, f32[1,1,256]{2,1,0:T(1,128)S(1)}, u32[]{:S(2)}) copy-start(f32[1,1,256]{2,1,0:T(1,128)S(1)} %get-tuple-element.88) | copy-start | bytes 3076
  55.7 30.8 %copy-start.20 = (f32[1,1,256]{2,1,0:T(1,128)}, f32[1,1,256]{2,1,0:T(1,128)S(1)}, u32[]{:S(2)}) copy-start(f32[1,1,256]{2,1,0:T(1,128)S(1)} %get-tuple-element.89) | copy-start | bytes 3076
  55.7 30.8 %copy-start.22 = (f32[1,1,256]{2,1,0:T(1,128)}, f32[1,1,256]{2,1,0:T(1,128)S(1)}, u32[]{:S(2)}) copy-start(f32[1,1,256]{2,1,0:T(1,128)S(1)} %get-tuple-element.90) | copy-start | bytes 3076
  55.7 30.8 %copy-start.24 = (f32[1,1,256]{2,1,0:T(1,128)}, f32[1,1,256]{2,1,0:T(1,128)S(1)}, u32[]{:S(2)}) copy-start(f32[1,1,256]{2,1,0:T(1,128)S(1)} %get-tuple-element.91) | copy-start | bytes 3076
  55.7 30.8 %copy-start.26 = (f32[1,1,256]{2,1,0:T(1,128)}, f32[1,1,256]{2,1,0:T(1,128)S(1)}, u32[]{:S(2)}) copy-start(f32[1,1,256]{2,1,0:T(1,128)S(1)} %get-tuple-element.92) | copy-start | bytes 3076
  55.7 30.8 %copy-start.28 = (f32[1,1,256]{2,1,0:T(1,128)}, f32[1,1,256]{2,1,0:T(1,128)S(1)}, u32[]{:S(2)}) copy-start(f32[1,1,256]{2,1,0:T(1,128)S(1)} %get-tuple-element.93) | copy-start | bytes 3076
  77.1 9.4 %copy-start.8 = (bf16[1,1024,256]{1,2,0:T(8,128)(2,1)}, bf16[1,1024,256]{1,2,0:T(8,128)(2,1)S(1)}, u32[]{:S(2)}) copy-start(bf16[1,1024,256]{1,2,0:T(8,128)(2,1)S(1)} %collective-permute-done) | copy-start | bytes 1572868
  77.1 9.5 %copy-start.9 = (bf16[1,1024,256]{1,2,0:T(8,128)(2,1)}, bf16[1,1024,256]{1,2,0:T(8,128)(2,1)S(1)}, u32[]{:S(2)}) copy-start(bf16[1,1024,256]{1,2,0:T(8,128)(2,1)S(1)} %collective-permute-done.1) | copy-start | bytes 1572868
  79.6 7.0 %copy-start.2 = (bf16[6,1026,256]{1,2,0:T(8,128)(2,1)}, bf16[6,1026,256]{1,2,0:T(8,128)(2,1)S(1)}, u32[]{:S(2)}) copy-start(bf16[6,1026,256]{1,2,0:T(8,128)(2,1)S(1)} %select_maximum_fusion.3) | copy-start | bytes 9455620
  79.6 8.3 %copy-start.38 = (bf16[1024,1024,1]{1,0,2:T(8,128)(2,1)S(1)}, bf16[1024,1024,1]{1,0,2:T(8,128)(2,1)}, u32[]{:S(2)}) copy-start(bf16[1024,1024,1]{1,0,2:T(8,128)(2,1)} %constant.45) | copy-start | bytes 6291460
  86.6 1.3 copy-start.10
  89.2 8.0 %copy-start.11 = (bf16[4,1024,128]{2,1,0:T(8,128)(2,1)S(1)}, bf16[4,1024,128]{2,1,0:T(8,128)(2,1)}, u32[]{:S(2)}) copy-start(bf16[4,1024,128]{2,1,0:T(8,128)(2,1)} %param.17) | copy-start | bytes 3145732
  90.7 32.5 %all-to-all-start = ((bf16[4,1024,128]{2,0,1:T(4,128)(2,1)}), bf16[4,1024,128]{2,0,1:T(4,128)(2,1)S(1)}, u32[]{:S(2)}, u32[]{:S(2)}) async-start(bf16[4,1024,128]{2,0,1:T(4,128)(2,1)} %copy.52), calls=%async_computation | async-start | bytes 2097152 | tf_op jit(solution)/shard_map/all_to_all | solution.py:118
  102.0 26.4 %copy-start.31 = (bf16[32,128]{1,0:T(8,128)(2,1)S(1)}, bf16[32,128]{1,0:T(8,128)(2,1)}, u32[]{:S(2)}) copy-start(bf16[32,128]{1,0:T(8,128)(2,1)} %param.16) | copy-start | bytes 24580
  102.0 26.4 %copy-start.32 = (bf16[32,32]{0,1:T(8,128)(2,1)S(1)}, bf16[32,32]{0,1:T(8,128)(2,1)}, u32[]{:S(2)}) copy-start(bf16[32,32]{0,1:T(8,128)(2,1)} %constant.32.clone) | copy-start | bytes 6148
  123.1 29.9 %all-to-all-start.2 = ((bf16[4,1024,128]{2,0,1:T(4,128)(2,1)}), bf16[4,1024,128]{2,0,1:T(4,128)(2,1)}, u32[]{:S(2)}, u32[]{:S(2)}) async-start(bf16[4,1024,128]{2,0,1:T(4,128)(2,1)} %copy.58), calls=%async_computation.2 | async-start | bytes 2097152 | tf_op jit(solution)/shard_map/all_to_all | solution.py:118
  127.6 26.8 %copy-start.30 = (bf16[32,32,1]{0,1,2:T(8,128)(2,1)S(1)}, bf16[32,32,1]{0,1,2:T(8,128)(2,1)}, u32[]{:S(2)}) copy-start(bf16[32,32,1]{0,1,2:T(8,128)(2,1)} %constant.46) | copy-start | bytes 6148
  128.3 29.7 %copy-start.33 = (f32[128]{0:T(128)}, f32[128]{0:T(128)S(1)}, u32[]{:S(2)}) copy-start(f32[128]{0:T(128)S(1)} %dynamic_slice.7) | copy-start | bytes 1540
  128.4 1.9 copy-start.36
  154.4 1.0 copy-start.14
  158.4 1.1 copy-start.34
  161.5 29.3 %all-to-all-start.1 = ((bf16[32,128,128]{2,1,0:T(8,128)(2,1)}), bf16[32,128,128]{2,1,0:T(8,128)(2,1)S(1)}, u32[]{:S(2)}, u32[]{:S(2)}) async-start(bf16[32,128,128]{2,1,0:T(8,128)(2,1)} %copy.55), calls=%async_computation.1 | async-start | bytes 2097152 | tf_op jit(solution)/shard_map/all_to_all | solution.py:122
  190.8 29.6 %all-to-all-start.3 = ((bf16[32,128,128]{2,1,0:T(8,128)(2,1)}), bf16[32,128,128]{2,1,0:T(8,128)(2,1)S(1)}, u32[]{:S(2)}, u32[]{:S(2)}) async-start(bf16[32,128,128]{2,1,0:T(8,128)(2,1)} %copy.62), calls=%async_computation.3 | async-start | bytes 2097152 | tf_op jit(solution)/shard_map/all_to_all | solution.py:122
  194.4 137.1 %reduce-scatter.4.cloned.1.call-start = ((), (), s32[]{:S(2)}) async-start(), calls=%async_computation.7 | async-start | bytes 5242880
  201.3 61.0 %copy-start.5 = (bf16[4,1024,128]{1,2,0:T(8,128)(2,1)}, bf16[4,1024,128]{1,2,0:T(8,128)(2,1)S(1)}, u32[]{:S(2)}) copy-start(bf16[4,1024,128]{1,2,0:T(8,128)(2,1)S(1)} %get-tuple-element.65) | copy-start | bytes 3145732
  224.4 37.9 %copy-start.6 = (bf16[4,1024,128]{1,2,0:T(8,128)(2,1)}, bf16[4,1024,128]{1,2,0:T(8,128)(2,1)S(1)}, u32[]{:S(2)}) copy-start(bf16[4,1024,128]{1,2,0:T(8,128)(2,1)S(1)} %fusion.34) | copy-start | bytes 3145732
  224.5 29.0 %copy-start.17 = (f32[1,1,256]{2,1,0:T(1,128)S(1)}, f32[1,1,256]{2,1,0:T(1,128)}, u32[]{:S(2)}) copy-start(f32[1,1,256]{2,1,0:T(1,128)} %copy-done.16) | copy-start | bytes 3076
  224.6 29.0 %copy-start.19 = (f32[1,1,256]{2,1,0:T(1,128)S(1)}, f32[1,1,256]{2,1,0:T(1,128)}, u32[]{:S(2)}) copy-start(f32[1,1,256]{2,1,0:T(1,128)} %copy-done.18) | copy-start | bytes 3076
  224.6 29.0 %copy-start.21 = (f32[1,1,256]{2,1,0:T(1,128)S(1)}, f32[1,1,256]{2,1,0:T(1,128)}, u32[]{:S(2)}) copy-start(f32[1,1,256]{2,1,0:T(1,128)} %copy-done.20) | copy-start | bytes 3076
  224.6 29.0 %copy-start.23 = (f32[1,1,256]{2,1,0:T(1,128)S(1)}, f32[1,1,256]{2,1,0:T(1,128)}, u32[]{:S(2)}) copy-start(f32[1,1,256]{2,1,0:T(1,128)} %copy-done.22) | copy-start | bytes 3076
  224.6 29.0 %copy-start.25 = (f32[1,1,256]{2,1,0:T(1,128)S(1)}, f32[1,1,256]{2,1,0:T(1,128)}, u32[]{:S(2)}) copy-start(f32[1,1,256]{2,1,0:T(1,128)} %copy-done.24) | copy-start | bytes 3076
  224.6 29.0 %copy-start.27 = (f32[1,1,256]{2,1,0:T(1,128)S(1)}, f32[1,1,256]{2,1,0:T(1,128)}, u32[]{:S(2)}) copy-start(f32[1,1,256]{2,1,0:T(1,128)} %copy-done.26) | copy-start | bytes 3076
  224.6 29.0 %copy-start.29 = (f32[1,1,256]{2,1,0:T(1,128)S(1)}, f32[1,1,256]{2,1,0:T(1,128)}, u32[]{:S(2)}) copy-start(f32[1,1,256]{2,1,0:T(1,128)} %copy-done.28) | copy-start | bytes 3076
  224.6 25.1 %collective-permute-start.2 = (bf16[1,1024,256]{1,2,0:T(8,128)(2,1)S(1)}, bf16[1,1024,256]{1,2,0:T(8,128)(2,1)S(1)}, u32[]{:S(2)}, u32[]{:S(2)}) collective-permute-start(bf16[1,1024,256]{1,2,0:T(8,128)(2,1)S(1)} %get-tuple-element.63), channel_id=1, source_target_pairs={{0,4},{4,8},{8,12},{12,16},{16,20},{20,24},{24,28},{1,5},{5,9},{9,... | collective-permute-start | bytes 1572872 | tf_op jit(solution)/shard_map/ppermute | solution.py:75
  228.1 21.6 %collective-permute-start.3 = (bf16[1,1024,256]{1,2,0:T(8,128)(2,1)S(1)}, bf16[1,1024,256]{1,2,0:T(8,128)(2,1)S(1)}, u32[]{:S(2)}, u32[]{:S(2)}) collective-permute-start(bf16[1,1024,256]{1,2,0:T(8,128)(2,1)S(1)} %get-tuple-element.64), channel_id=1, source_target_pairs={{4,0},{8,4},{12,8},{16,12},{20,16},{24,20},{28,24},{5,1},{9,5},{13... | collective-permute-start | bytes 1572872 | tf_op jit(solution)/shard_map/ppermute | solution.py:76
  262.3 1.3 copy-start.7
  281.6 4.8 %copy-start.3 = (bf16[6,1026,256]{1,2,0:T(8,128)(2,1)S(1)}, bf16[6,1026,256]{1,2,0:T(8,128)(2,1)}, u32[]{:S(2)}) copy-start(bf16[6,1026,256]{1,2,0:T(8,128)(2,1)} %copy-done.2) | copy-start | bytes 9455620
  298.7 5.1 %copy-start.13 = (bf16[1024,128]{1,0:T(8,128)(2,1)S(1)}, bf16[1024,128]{1,0:T(8,128)(2,1)}, u32[]{:S(2)}) copy-start(bf16[1024,128]{1,0:T(8,128)(2,1)} %fusion.38) | copy-start | bytes 786436
  303.5 9.7 %copy-start.12 = (bf16[4,1024,128]{1,2,0:T(8,128)(2,1)S(1)}, bf16[4,1024,128]{1,2,0:T(8,128)(2,1)}, u32[]{:S(2)}) copy-start(bf16[4,1024,128]{1,2,0:T(8,128)(2,1)} %get-tuple-element.66) | copy-start | bytes 3145732
  308.0 21.0 %all-to-all-start.4 = ((bf16[8,278,128]{2,1,0:T(8,128)(2,1)}), bf16[8,278,128]{2,1,0:T(8,128)(2,1)S(1)}, u32[]{:S(2)}, u32[]{:S(2)}) async-start(bf16[8,278,128]{2,1,0:T(8,128)(2,1)} %concatenate.70), calls=%async_computation.4 | async-start | bytes 1146880 | tf_op jit(solution)/shard_map/all_to_all | solution.py:184
  313.2 21.9 %copy-start.1 = (bf16[1024,128]{1,0:T(8,128)(2,1)S(1)}, bf16[1024,128]{1,0:T(8,128)(2,1)}, u32[]{:S(2)}) copy-start(bf16[1024,128]{1,0:T(8,128)(2,1)} %param.15) | copy-start | bytes 786436
  (2 other events, 1.5 us)
Sparse Core Ops, SparseCore 0:
  9.6 37.7 all-gather.1
  281.7 44.6 reduce-scatter.3
